TPU v7x, 32 devices: a whole 2x2x4 slice. The times are simulated.
32 devices in a mesh: space: 8 (over y, x, core), angle: 4 (over z).
Axes of the slice: x: 2, y: 2, z: 4, core: 2. Of those that a mesh axis runs over, the one named last changes fastest.
Arguments:
- phase_delay: float32 [2, 256, 2048], P(None, 'space'), may hold values from -6 to 6
- measured: float32 [4, 2, 256, 2048], P('angle', None, 'space'), may hold values from -6 to 6
- tilts: float32 [4, 2], P('angle'), may hold values from -0.4 to 0.4
- fresnel_taps: float32 [2, 2, 33], replicated, may hold values from -0.75 to 0.75
Outputs:
- gradient: float32 [2, 256, 2048], P(None, 'space', 'angle')
All inputs are finite; a program needn't handle non-finite values.
Results may differ from a plain program's by a relative error of at most 0.0003.
Values sent between devices are 32-bit elements; how exact they have to be, the bound alone decides.
A program may use at most 64 MiB of HBM per device.

v0:
```python
import jax
import jax.numpy as jnp
from jax import lax
from jax.sharding import PartitionSpec as P

tile_width = 128
highest = lax.Precision.HIGHEST


def padded_2(block, sides, width):
    for axis, dim in sides:
        count = lax.axis_size(axis)
        forward = [(i, i + 1) for i in range(count - 1)]
        backward = [(target, source) for source, target in forward]
        low = lax.ppermute(
            lax.slice_in_dim(block, block.shape[dim] - width, None, axis=dim), axis, forward
        )
        high = lax.ppermute(lax.slice_in_dim(block, 0, width, axis=dim), axis, backward)
        block = jnp.concatenate([low, block, high], axis=dim)
    return block


def adjoint_kernel(kernel):
    return jnp.stack([kernel[0, ::-1], -kernel[1, ::-1]])


def tap_table(kernel, offsets):
    tap_count = kernel.shape[1]
    onehot = (offsets[None] == jnp.arange(tap_count, dtype=jnp.int32)[:, None, None]).astype(
        jnp.float32
    )
    return jnp.einsum("ck,kij->cij", kernel, onehot, precision=highest)


def band_blocks(kernel):
    reach = (kernel.shape[1] - 1) // 2
    source = lax.broadcasted_iota(jnp.int32, (tile_width, tile_width), 0)
    target = lax.broadcasted_iota(jnp.int32, (tile_width, tile_width), 1)
    stacked = []
    for block_shift in (-1, 0, 1):
        table = tap_table(kernel, target - source - tile_width * block_shift + reach)
        real_row = jnp.stack([table[0], table[1]], axis=1)
        imag_row = jnp.stack([-table[1], table[0]], axis=1)
        stacked.append(jnp.stack([real_row, imag_row]))
    return jnp.stack(stacked)


def row_matrix(kernel, out_rows):
    reach = (kernel.shape[1] - 1) // 2
    out_index = lax.broadcasted_iota(jnp.int32, (out_rows, out_rows + 2 * reach), 0)
    in_index = lax.broadcasted_iota(jnp.int32, (out_rows, out_rows + 2 * reach), 1)
    return tap_table(kernel, out_index + 2 * reach - in_index)


def complex_rows(padded, matrix):
    real_in = padded[..., 0, :, :]
    imag_in = padded[..., 1, :, :]
    real_out = jnp.einsum("xj,...jy->...xy", matrix[0], real_in, precision=highest) - jnp.einsum(
        "xj,...jy->...xy", matrix[1], imag_in, precision=highest
    )
    imag_out = jnp.einsum("xj,...jy->...xy", matrix[0], imag_in, precision=highest) + jnp.einsum(
        "xj,...jy->...xy", matrix[1], real_in, precision=highest
    )
    return jnp.stack([real_out, imag_out], axis=-3)


def complex_columns(wave_field, blocks):
    shape = wave_field.shape
    tile_count = shape[-1] // tile_width
    tiles = wave_field.reshape(shape[:-1] + (tile_count, tile_width))
    padding = [(0, 0)] * (tiles.ndim - 2) + [(1, 1), (0, 0)]
    tiles = jnp.pad(tiles, padding)
    total = None
    for position, block_shift in enumerate((-1, 0, 1)):
        source_tiles = tiles[..., 1 + block_shift : 1 + block_shift + tile_count, :]
        term = jnp.einsum(
            "...cxtk,ckdj->...dxtj", source_tiles, blocks[position], precision=highest
        )
        total = term if total is None else total + term
    return total.reshape(shape)


def transmit(wave_field, cosine, sine):
    real_in = wave_field[:, 0]
    imag_in = wave_field[:, 1]
    return jnp.stack([cosine * real_in - sine * imag_in, cosine * imag_in + sine * real_in], axis=1)


def release(wave_field, cosine, sine):
    real_in = wave_field[:, 0]
    imag_in = wave_field[:, 1]
    return jnp.stack([cosine * real_in + sine * imag_in, cosine * imag_in - sine * real_in], axis=1)


def incident(tilts, first_row, length, column_count):
    positions = (first_row + jnp.arange(length, dtype=jnp.int32)).astype(jnp.float32)
    columns_float = jnp.arange(column_count, dtype=jnp.float32)
    ramp = (
        tilts[:, 0, None, None] * positions[None, :, None]
        + tilts[:, 1, None, None] * columns_float[None, None, :]
    )
    return jnp.stack([jnp.cos(ramp), jnp.sin(ramp)], axis=1)


def body(phase_delay, measured, tilts, fresnel_taps):
    slice_count, strip_rows, column_count = phase_delay.shape
    reach = (fresnel_taps.shape[2] - 1) // 2
    first_row = lax.axis_index("space") * strip_rows
    column_blocks = band_blocks(fresnel_taps[1])
    column_back = band_blocks(adjoint_kernel(fresnel_taps[1]))
    cosines = jnp.cos(phase_delay)
    sines = jnp.sin(phase_delay)
    stored = []
    wave_field = incident(tilts, first_row, strip_rows, column_count)
    row_forward = row_matrix(fresnel_taps[0], strip_rows)
    for layer in range(slice_count):
        transmitted = transmit(wave_field, cosines[layer], sines[layer])
        stored.append(transmitted)
        padded = padded_2(transmitted, (("space", 2),), reach)
        wave_field = complex_columns(complex_rows(padded, row_forward), column_blocks)
    row_backward = row_matrix(adjoint_kernel(fresnel_taps[0]), strip_rows)
    backward = wave_field - measured
    terms = [None] * slice_count
    for layer in reversed(range(slice_count)):
        spread_field = complex_columns(backward, column_back)
        padded = padded_2(spread_field, (("space", 2),), reach)
        sensitivity = complex_rows(padded, row_backward)
        transmitted = stored[layer]
        terms[layer] = jnp.sum(
            transmitted[:, 0] * sensitivity[:, 1] - transmitted[:, 1] * sensitivity[:, 0], axis=0
        )
        if layer > 0:
            backward = release(sensitivity, cosines[layer], sines[layer])
    return lax.psum_scatter(jnp.stack(terms), "angle", scatter_dimension=2, tiled=True)


def solution(mesh):
    return jax.shard_map(
        body,
        mesh=mesh,
        in_specs=(P(None, "space", None), P("angle", None, "space", None), P("angle", None), P()),
        out_specs=P(None, "space", "angle"),
        check_vma=False,
    )
```

profile of v0, /device:TPU:0, one launch (start us, length us, event | category | flops | bytes accessed | tf_op | source)
XLA Modules:
  0.0 117.4 jit_solution(15728039494688761808)
XLA Ops:
  6.5 2.8 %fusion.135 = (f32[2,32,2048]{2,1,0:T(8,128)S(1)}, f32[2,32,2048]{2,1,0:T(8,128)S(1)}) fusion(f32[2,32,2048]{2,1,0:T(8,128)} %param.4), kind=kLoop, calls=%fused_computation.226 | loop fusion | bytes 1572864 | tf_op jit(solution)/shard_map/cos | solution.py:111
  11.2 1.2 fusion.129
  12.4 0.7 fusion.93
  13.1 3.1 %collective-permute-start = (f32[1,2,16,2048]{3,2,1,0:T(8,128)}, f32[1,2,16,2048]{3,2,1,0:T(8,128)}, u32[]{:S(2)}, u32[]{:S(2)}) collective-permute-start(f32[1,2,16,2048]{3,2,1,0:T(8,128)} %get-tuple-element.24), channel_id=1, source_target_pairs={{0,4},{4,8},{8,12},{12,16},{16,20},{20,24},{24,28},{1,5},{5,9},{9,... | collective-permute-start | bytes 786440 | tf_op jit(solution)/shard_map/ppermute | solution.py:15
  16.2 1.3 %collective-permute-start.1 = (f32[1,2,16,2048]{3,2,1,0:T(8,128)S(1)}, f32[1,2,16,2048]{3,2,1,0:T(8,128)}, u32[]{:S(2)}, u32[]{:S(2)}) collective-permute-start(f32[1,2,16,2048]{3,2,1,0:T(8,128)S(1)} %get-tuple-element.25), channel_id=1, source_target_pairs={{4,0},{8,4},{12,8},{16,12},{20,16},{24,20},{28,24},{5,1},{9,5},{13... | collective-permute-start | bytes 786440 | tf_op jit(solution)/shard_map/ppermute | solution.py:18
  17.5 1.0 fusion.36
  18.5 1.0 fusion.37
  19.7 0.9 fusion.2
  20.6 0.9 fusion
  21.5 1.0 fusion.35
  22.5 0.9 fusion.5
  24.7 1.1 pad_maximum_fusion
  30.2 0.7 fusion.92
  30.9 5.1 %collective-permute-start.2 = (f32[1,2,16,2048]{3,2,1,0:T(8,128)}, f32[1,2,16,2048]{3,2,1,0:T(8,128)}, u32[]{:S(2)}, u32[]{:S(2)}) collective-permute-start(f32[1,2,16,2048]{3,2,1,0:T(8,128)} %get-tuple-element.20), channel_id=1, source_target_pairs={{0,4},{4,8},{8,12},{12,16},{16,20},{20,24},{24,28},{1,5},{5,9},{9,... | collective-permute-start | bytes 786440 | tf_op jit(solution)/shard_map/ppermute | solution.py:15
  36.1 1.5 %collective-permute-start.3 = (f32[1,2,16,2048]{3,2,1,0:T(8,128)S(1)}, f32[1,2,16,2048]{3,2,1,0:T(8,128)}, u32[]{:S(2)}, u32[]{:S(2)}) collective-permute-start(f32[1,2,16,2048]{3,2,1,0:T(8,128)S(1)} %get-tuple-element.21), channel_id=1, source_target_pairs={{4,0},{8,4},{12,8},{16,12},{20,16},{24,20},{28,24},{5,1},{9,5},{13... | collective-permute-start | bytes 786440 | tf_op jit(solution)/shard_map/ppermute | solution.py:18
  37.8 2.3 %collective-permute-done.3 = f32[1,2,16,2048]{3,2,1,0:T(8,128)} collective-permute-done((f32[1,2,16,2048]{3,2,1,0:T(8,128)S(1)}, f32[1,2,16,2048]{3,2,1,0:T(8,128)}, u32[]{:S(2)}, u32[]{:S(2)}) %collective-permute-start.3) | collective-permute-done | bytes 262176 | tf_op jit(solution)/shard_map/ppermute | solution.py:18
  40.2 1.1 pad_maximum_fusion.1
  45.4 0.7 copy-done
  46.2 0.7 copy_subtract_fusion
  47.1 0.7 convolution_bitcast_fusion.4
  49.4 7.8 %collective-permute-start.4 = (f32[1,2,16,2048]{3,0,2,1:T(1,128)S(1)}, f32[1,2,16,2048]{3,0,2,1:T(1,128)S(1)}, u32[]{:S(2)}, u32[]{:S(2)}) collective-permute-start(f32[1,2,16,2048]{3,0,2,1:T(1,128)S(1)} %get-tuple-element.18), channel_id=1, source_target_pairs={{0,4},{4,8},{8,12},{12,16},{16,20},{20,24},{24,28},{1,5},{5,9},{9,... | collective-permute-start | bytes 786440 | tf_op jit(solution)/shard_map/ppermute | solution.py:15
  57.2 1.5 %collective-permute-start.5 = (f32[1,2,16,2048]{3,0,2,1:T(1,128)S(1)}, f32[1,2,16,2048]{3,0,2,1:T(1,128)S(1)}, u32[]{:S(2)}, u32[]{:S(2)}) collective-permute-start(f32[1,2,16,2048]{3,0,2,1:T(1,128)S(1)} %get-tuple-element.19), channel_id=1, source_target_pairs={{4,0},{8,4},{12,8},{16,12},{20,16},{24,20},{28,24},{5,1},{9,5},{13... | collective-permute-start | bytes 786440 | tf_op jit(solution)/shard_map/ppermute | solution.py:18
  59.1 1.5 %collective-permute-done.5 = f32[1,2,16,2048]{3,0,2,1:T(1,128)S(1)} collective-permute-done((f32[1,2,16,2048]{3,0,2,1:T(1,128)S(1)}, f32[1,2,16,2048]{3,0,2,1:T(1,128)S(1)}, u32[]{:S(2)}, u32[]{:S(2)}) %collective-permute-start.5) | collective-permute-done | bytes 262176 | tf_op jit(solution)/shard_map/ppermute | solution.py:18
  60.6 0.9 pad_maximum_fusion.2
  66.5 6.9 %collective-permute-start.6 = (f32[1,2,16,2048]{3,0,2,1:T(1,128)S(1)}, f32[1,2,16,2048]{3,0,2,1:T(1,128)S(1)}, u32[]{:S(2)}, u32[]{:S(2)}) collective-permute-start(f32[1,2,16,2048]{3,0,2,1:T(1,128)S(1)} %get-tuple-element.15), channel_id=1, source_target_pairs={{0,4},{4,8},{8,12},{12,16},{16,20},{20,24},{24,28},{1,5},{5,9},{9,... | collective-permute-start | bytes 786440 | tf_op jit(solution)/shard_map/ppermute | solution.py:15
  73.4 1.3 %collective-permute-start.7 = (f32[1,2,16,2048]{3,0,2,1:T(1,128)S(1)}, f32[1,2,16,2048]{3,0,2,1:T(1,128)S(1)}, u32[]{:S(2)}, u32[]{:S(2)}) collective-permute-start(f32[1,2,16,2048]{3,0,2,1:T(1,128)S(1)} %get-tuple-element.16), channel_id=1, source_target_pairs={{4,0},{8,4},{12,8},{16,12},{20,16},{24,20},{28,24},{5,1},{9,5},{13... | collective-permute-start | bytes 786440 | tf_op jit(solution)/shard_map/ppermute | solution.py:18
  74.7 2.1 %collective-permute-done.7 = f32[1,2,16,2048]{3,0,2,1:T(1,128)S(1)} collective-permute-done((f32[1,2,16,2048]{3,0,2,1:T(1,128)S(1)}, f32[1,2,16,2048]{3,0,2,1:T(1,128)S(1)}, u32[]{:S(2)}, u32[]{:S(2)}) %collective-permute-start.7) | collective-permute-done | bytes 262176 | tf_op jit(solution)/shard_map/ppermute | solution.py:18
  76.8 0.9 pad_maximum_fusion.3
  79.0 1.5 %fusion.12 = f32[1,32,2048]{2,1,0:T(8,128)S(1)} fusion(f32[2048,32]{0,1:T(8,128)S(1)} %fusion.55, f32[32,64]{1,0:T(8,128)S(1)} %bitcast.447, f32[1,1,64,2048]{3,0,2,1:T(1,128)S(1)} %get-tuple-element.11, f32[2,32,2048]{2,1,0:T(8,128)S(1)} %get-tuple-element.27, f32[2048]{0:T(1024)S(1)} %iota_multiply_fusion, f32[32]{0:T(128)S(1)} %convert_multiply_fusion, ...), kind=kOutput, calls=%fused_computation.23 | convolution fusion | flops 50724864 | bytes 1589376 | tf_op jit(solution)/shard_map/xj,...jy->...xy/dot_general | solution.py:58
  80.4 1.5 %fusion.11 = f32[1,32,2048]{2,1,0:T(8,128)S(1)} fusion(f32[1,32,2048]{2,1,0:T(8,128)S(1)} %fusion.12, f32[2048,32]{0,1:T(8,128)S(1)} %fusion.59, f32[32,64]{1,0:T(8,128)S(1)} %bitcast.448, f32[1,1,64,2048]{3,0,2,1:T(1,128)S(1)} %get-tuple-element.12, f32[2,32,2048]{2,1,0:T(8,128)S(1)} %get-tuple-element.27, f32[2048]{0:T(1024)S(1)} %iota_multiply_fusion, ...), kind=kOutput, calls=%fused_computation.22 | convolution fusion | flops 50790400 | bytes 1851520 | tf_op jit(solution)/shard_map/xj,...jy->...xy/dot_general | solution.py:61
  81.9 0.8 pad_maximum_fusion.4
  82.8 27.7 %reduce-scatter.2.cloned.1.call-done = f32[2,32,512]{2,1,0:T(8,128)} async-done(((f32[2,32,2048]{2,1,0:T(8,128)}), f32[2,32,512]{2,1,0:T(8,128)}) %reduce-scatter.2.cloned.1.call-update) | async-done | bytes 131088 | tf_op jit(solution)/shard_map/reduce_scatter | solution.py:134
  (97 shorter events, 19.9 us)
Async XLA Ops:
  6.5 2.8 %copy-start.2 = (f32[1,2]{1,0:T(1,128)S(1)}, f32[1,2]{1,0:T(1,128)}, u32[]{:S(2)}) copy-start(f32[1,2]{1,0:T(1,128)} %param.6) | copy-start | bytes 28
  6.5 104.0 %reduce-scatter.2.cloned.1.call-start = ((), (), s32[]{:S(2)}) async-start(), calls=%async_computation.1 | async-start | bytes 655360 | tf_op jit(solution)/shard_map/reduce_scatter | solution.py:134
  11.2 6.3 %copy-start.1 = (f32[2,2,33]{2,1,0:T(2,128)S(1)}, f32[2,2,33]{2,1,0:T(2,128)}, u32[]{:S(2)}) copy-start(f32[2,2,33]{2,1,0:T(2,128)} %param.7) | copy-start | bytes 1588
  13.1 11.6 %collective-permute-start = (f32[1,2,16,2048]{3,2,1,0:T(8,128)}, f32[1,2,16,2048]{3,2,1,0:T(8,128)}, u32[]{:S(2)}, u32[]{:S(2)}) collective-permute-start(f32[1,2,16,2048]{3,2,1,0:T(8,128)} %get-tuple-element.24), channel_id=1, source_target_pairs={{0,4},{4,8},{8,12},{12,16},{16,20},{20,24},{24,28},{1,5},{5,9},{9,... | collective-permute-start | bytes 786440 | tf_op jit(solution)/shard_map/ppermute | solution.py:15
  16.2 8.5 %collective-permute-start.1 = (f32[1,2,16,2048]{3,2,1,0:T(8,128)S(1)}, f32[1,2,16,2048]{3,2,1,0:T(8,128)}, u32[]{:S(2)}, u32[]{:S(2)}) collective-permute-start(f32[1,2,16,2048]{3,2,1,0:T(8,128)S(1)} %get-tuple-element.25), channel_id=1, source_target_pairs={{4,0},{8,4},{12,8},{16,12},{20,16},{24,20},{28,24},{5,1},{9,5},{13... | collective-permute-start | bytes 786440 | tf_op jit(solution)/shard_map/ppermute | solution.py:18
  30.9 6.9 %collective-permute-start.2 = (f32[1,2,16,2048]{3,2,1,0:T(8,128)}, f32[1,2,16,2048]{3,2,1,0:T(8,128)}, u32[]{:S(2)}, u32[]{:S(2)}) collective-permute-start(f32[1,2,16,2048]{3,2,1,0:T(8,128)} %get-tuple-element.20), channel_id=1, source_target_pairs={{0,4},{4,8},{8,12},{12,16},{16,20},{20,24},{24,28},{1,5},{5,9},{9,... | collective-permute-start | bytes 786440 | tf_op jit(solution)/shard_map/ppermute | solution.py:15
  36.1 4.1 %collective-permute-start.3 = (f32[1,2,16,2048]{3,2,1,0:T(8,128)S(1)}, f32[1,2,16,2048]{3,2,1,0:T(8,128)}, u32[]{:S(2)}, u32[]{:S(2)}) collective-permute-start(f32[1,2,16,2048]{3,2,1,0:T(8,128)S(1)} %get-tuple-element.21), channel_id=1, source_target_pairs={{4,0},{8,4},{12,8},{16,12},{20,16},{24,20},{28,24},{5,1},{9,5},{13... | collective-permute-start | bytes 786440 | tf_op jit(solution)/shard_map/ppermute | solution.py:18
  45.1 1.0 copy-start
  49.4 9.7 %collective-permute-start.4 = (f32[1,2,16,2048]{3,0,2,1:T(1,128)S(1)}, f32[1,2,16,2048]{3,0,2,1:T(1,128)S(1)}, u32[]{:S(2)}, u32[]{:S(2)}) collective-permute-start(f32[1,2,16,2048]{3,0,2,1:T(1,128)S(1)} %get-tuple-element.18), channel_id=1, source_target_pairs={{0,4},{4,8},{8,12},{12,16},{16,20},{20,24},{24,28},{1,5},{5,9},{9,... | collective-permute-start | bytes 786440 | tf_op jit(solution)/shard_map/ppermute | solution.py:15
  57.2 3.4 %collective-permute-start.5 = (f32[1,2,16,2048]{3,0,2,1:T(1,128)S(1)}, f32[1,2,16,2048]{3,0,2,1:T(1,128)S(1)}, u32[]{:S(2)}, u32[]{:S(2)}) collective-permute-start(f32[1,2,16,2048]{3,0,2,1:T(1,128)S(1)} %get-tuple-element.19), channel_id=1, source_target_pairs={{4,0},{8,4},{12,8},{16,12},{20,16},{24,20},{28,24},{5,1},{9,5},{13... | collective-permute-start | bytes 786440 | tf_op jit(solution)/shard_map/ppermute | solution.py:18
  66.5 8.2 %collective-permute-start.6 = (f32[1,2,16,2048]{3,0,2,1:T(1,128)S(1)}, f32[1,2,16,2048]{3,0,2,1:T(1,128)S(1)}, u32[]{:S(2)}, u32[]{:S(2)}) collective-permute-start(f32[1,2,16,2048]{3,0,2,1:T(1,128)S(1)} %get-tuple-element.15), channel_id=1, source_target_pairs={{0,4},{4,8},{8,12},{12,16},{16,20},{20,24},{24,28},{1,5},{5,9},{9,... | collective-permute-start | bytes 786440 | tf_op jit(solution)/shard_map/ppermute | solution.py:15
  73.4 3.4 %collective-permute-start.7 = (f32[1,2,16,2048]{3,0,2,1:T(1,128)S(1)}, f32[1,2,16,2048]{3,0,2,1:T(1,128)S(1)}, u32[]{:S(2)}, u32[]{:S(2)}) collective-permute-start(f32[1,2,16,2048]{3,0,2,1:T(1,128)S(1)} %get-tuple-element.16), channel_id=1, source_target_pairs={{4,0},{8,4},{12,8},{16,12},{20,16},{24,20},{28,24},{5,1},{9,5},{13... | collective-permute-start | bytes 786440 | tf_op jit(solution)/shard_map/ppermute | solution.py:18
Sparse Core Ops, SparseCore 0:
  82.9 27.5 reduce-scatter.1
where the time goes:
time: 118 us; the launch traced here: 117 us
  waiting for transfers between devices  33.8 us (29%)
  starting transfers between devices  28.5 us (24%)
  matrix products  23.4 us (20%)
  between operations  14.2 us (12%)
  other arithmetic  9.96 us (8%)
  local copies, waits for them, and re-layouts  7.62 us (6%)
    reduce_scatter x1, waiting for transfers between devices, body(): lax.psum_scatter(jnp.stack(terms), 'angle', scatter_dimension=2, tiled=True)  27.7 us
    ppermute x4, starting transfers between devices, padded_2(): lax.ppermute(lax.slice_in_dim(block, block.shape[dim] - width, None, axis...  22.9 us
    dot_general x12, matrix products, complex_columns(): jnp.einsum('...cxtk,ckdj->...dxtj', source_tiles, blocks[position], preci...  7.3 us
    dot_general x8, matrix products, tap_table(): return jnp.einsum('ck,kij->cij', kernel, onehot, precision=highest)  6.31 us
    ppermute x4, waiting for transfers between devices, padded_2(): lax.ppermute(lax.slice_in_dim(block, 0, width, axis=dim), axis, backward)  6.01 us
    ppermute x4, starting transfers between devices, padded_2(): lax.ppermute(lax.slice_in_dim(block, 0, width, axis=dim), axis, backward)  5.55 us
    concatenate x4, other arithmetic, padded_2(): block = jnp.concatenate([low, block, high], axis=dim)  4.06 us
    dot_general x4, matrix products, complex_rows(): jnp.einsum('xj,...jy->...xy', matrix[1], imag_in, precision=highest)  2.97 us
  transfers between devices with their start and end apart: 9, of which 4 were waited for; matrix products, arithmetic and copies ran while one was open for 7% of the time, Pallas kernels for 0%

commit v1 on v0

v1 whole, which is shorter than its diff:
```python
import functools

import jax
import jax.numpy as jnp
from jax import lax
from jax.experimental import pallas as pl
from jax.experimental.pallas import tpu as pltpu
from jax.sharding import PartitionSpec as P

LANES = 128
MESH = pl.DeviceIdType.MESH
f32 = jnp.float32
bf16 = jnp.bfloat16


def sincos(x):
    k = jnp.floor(x * f32(0.3183098861837907) + f32(0.5))
    r = ((x - k * f32(3.140625)) - k * f32(9.67502593994140625e-4)) - k * f32(1.509957990978376e-7)
    sign = f32(1.0) - f32(2.0) * (k - f32(2.0) * jnp.floor(k * f32(0.5)))
    z = r * r
    s = f32(-2.5052108e-8)
    for c in (2.7557319e-6, -1.9841270e-4, 8.3333333e-3, -1.6666667e-1, 1.0):
        s = s * z + f32(c)
    c_ = f32(2.0876757e-9)
    for c in (-2.7557319e-7, 2.4801587e-5, -1.3888889e-3, 4.1666667e-2, -0.5, 1.0):
        c_ = c_ * z + f32(c)
    return sign * s * r, sign * c_


def split(x):
    hi = x.astype(bf16)
    return hi, (x - hi.astype(f32)).astype(bf16)


def kernel(
    sizes, phase, meas, tilts, taps, out,
    p0h, p1h, erow, ecol, t1s, w0s, w1s, zah, zal, zbh, zbl, zch, zcl, zdh, zdl,
    wf, wb, rf64, rf32, rb64, rb32, lam, lamh, gs, rsr,
    p0_send, p0_recv, p1_send, p1_recv, l_send, l_recv, g_send, g_recv,
):
    n_space, n_angle, chunks = sizes
    rows, cols = phase.shape[1], phase.shape[2]
    n_taps = taps.shape[2]
    reach = (n_taps - 1) // 2
    wide = rows + 2 * reach
    widest = rows + 4 * reach
    blocks = cols // LANES
    per = blocks // chunks
    piece = blocks // n_angle
    pieces_per_chunk = n_angle // chunks
    width = per * LANES
    s = lax.axis_index("space")
    q = lax.axis_index("angle")
    has_up = s > 0
    has_dn = s < n_space - 1
    up_id = (jnp.maximum(s - 1, 0), q)
    dn_id = (jnp.minimum(s + 1, n_space - 1), q)

    barrier = pltpu.get_barrier_semaphore()

    @pl.when(has_up)
    def _():
        pl.semaphore_signal(barrier, inc=1, device_id=up_id, device_id_type=MESH)

    @pl.when(has_dn)
    def _():
        pl.semaphore_signal(barrier, inc=1, device_id=dn_id, device_id_type=MESH)

    for j in range(n_angle):
        @pl.when(q != j)
        def _():
            pl.semaphore_signal(barrier, inc=1, device_id=(s, jnp.int32(j)), device_id_type=MESH)

    expected = n_angle - 1 + jnp.where(has_up, 1, 0) + jnp.where(has_dn, 1, 0)
    pl.semaphore_wait(barrier, expected)

    def p0_copy(side, c):
        at = pl.ds(c * width, width)
        return pltpu.make_async_remote_copy(
            phase.at[0, :, at], p0h.at[side, :, at], p0_send.at[side, c], p0_recv.at[side, c],
            device_id=dn_id if side == 0 else up_id, device_id_type=MESH)

    def p1_copy(side, c):
        at = pl.ds(c * width, width)
        first = rows - reach if side == 0 else 0
        return pltpu.make_async_remote_copy(
            phase.at[1, pl.ds(first, reach), at], p1h.at[side, :, at], p1_send.at[side, c], p1_recv.at[side, c],
            device_id=dn_id if side == 0 else up_id, device_id_type=MESH)

    def l_copy(side, c):
        at = pl.ds(c * per, per)
        return pltpu.make_async_remote_copy(
            lam.at[at], lamh.at[side, at], l_send.at[side, c], l_recv.at[side, c],
            device_id=dn_id if side == 0 else up_id, device_id_type=MESH)

    def g_copy(k, p):
        return pltpu.make_async_remote_copy(
            gs.at[k, pl.ds(p * piece, piece)], rsr.at[q, k], g_send.at[k, p], g_recv.at[k, q],
            device_id=(s, jnp.int32(p)), device_id_type=MESH)

    def g_arrival(k, j):
        return pltpu.make_async_remote_copy(
            gs.at[k, pl.ds(0, piece)], rsr.at[j, k], g_send.at[k, 0], g_recv.at[k, j],
            device_id=(s, jnp.int32(j)), device_id_type=MESH)

    def sending(make):
        @pl.when(has_dn)
        def _():
            make(0).start()

        @pl.when(has_up)
        def _():
            make(1).start()

    def arriving(make):
        @pl.when(has_up)
        def _():
            make(0).wait_recv()

        @pl.when(has_dn)
        def _():
            make(1).wait_recv()

    def sent(make):
        @pl.when(has_dn)
        def _():
            make(0).wait_send()

        @pl.when(has_up)
        def _():
            make(1).wait_send()

    for c in range(chunks):
        sending(lambda side: p0_copy(side, c))
        sending(lambda side: p1_copy(side, c))

    @pl.when(jnp.logical_not(has_up))
    def _():
        p0h[0] = jnp.zeros(p0h.shape[1:], f32)
        p1h[0] = jnp.zeros(p1h.shape[1:], f32)
        lamh[0] = jnp.zeros(lamh.shape[1:], f32)

    @pl.when(jnp.logical_not(has_dn))
    def _():
        p0h[1] = jnp.zeros(p0h.shape[1:], f32)
        p1h[1] = jnp.zeros(p1h.shape[1:], f32)
        lamh[1] = jnp.zeros(lamh.shape[1:], f32)

    for ref in (zah, zal, zbh, zbl, zch, zcl, zdh, zdl):
        ref[0] = jnp.zeros(ref.shape[1:], bf16)
        ref[blocks + 1] = jnp.zeros(ref.shape[1:], bf16)

    src = lax.broadcasted_iota(jnp.int32, (LANES, LANES), 0)
    dst = lax.broadcasted_iota(jnp.int32, (LANES, LANES), 1)
    away = dst - src
    turn = jnp.bitwise_and(away + LANES, LANES - 1)
    r_out = lax.broadcasted_iota(jnp.int32, (wide, LANES), 0)
    r_in = lax.broadcasted_iota(jnp.int32, (wide, LANES), 1)
    r_away = r_out + reach - r_in

    def build(step, carry):
        cr, ci, br, bi, rr, ri, ar, ai = carry
        a = step - reach
        hr, hi = taps[1, 0, step], taps[1, 1, step]
        gr, gi = taps[0, 0, step], taps[0, 1, step]
        here = turn == jnp.bitwise_and(a + LANES, LANES - 1)
        there = turn == jnp.bitwise_and(LANES - a, LANES - 1)
        r_here = r_away == a
        r_there = r_away == -a
        return (
            jnp.where(here, hr, cr), jnp.where(here, hi, ci),
            jnp.where(there, hr, br), jnp.where(there, -hi, bi),
            jnp.where(r_here, gr, rr), jnp.where(r_here, gi, ri),
            jnp.where(r_there, gr, ar), jnp.where(r_there, -gi, ai),
        )

    zc = jnp.zeros((LANES, LANES), f32)
    zr = jnp.zeros((wide, LANES), f32)
    cr, ci, br, bi, rr, ri, ar, ai = lax.fori_loop(
        0, n_taps, build, (zc, zc, zc, zc, zr, zr, zr, zr))
    masks = (away <= reach - LANES, jnp.abs(away) <= reach, away >= LANES - reach)
    for table, real, imag in ((wf, cr, ci), (wb, br, bi)):
        for m, mask in enumerate(masks):
            re, im = jnp.where(mask, real, 0.0), jnp.where(mask, imag, 0.0)
            hi, lo = split(jnp.concatenate(
                [jnp.concatenate([re, im], axis=1), jnp.concatenate([-im, re], axis=1)], axis=0))
            table[pl.ds(256 * m, 256)] = hi
            table[pl.ds(256 * (m + 3), 256)] = hi
            table[pl.ds(256 * (m + 6), 256)] = lo
    for big, small, real, imag in ((rf64, rf32, rr, ri), (rb64, rb32, ar, ai)):
        rh, rl = split(real)
        ih, il = split(imag)
        big[...] = jnp.concatenate([rh, ih, rl, il], axis=0)[:, :widest]
        small[...] = jnp.concatenate([rh[:rows], ih[:rows], rl[:rows], il[:rows]], axis=0)[:, :wide]

    row_at = lax.broadcasted_iota(jnp.int32, (widest, LANES), 0)
    row_no = (s * rows - 2 * reach + row_at).astype(f32)
    es, ec = sincos(tilts[0, 0] * row_no)
    inside = jnp.where(row_at < 2 * reach, jnp.where(has_up, 1.0, 0.0),
                       jnp.where(row_at >= 2 * reach + rows, jnp.where(has_dn, 1.0, 0.0), 1.0)).astype(f32)
    erow[0] = ec * inside
    erow[1] = es * inside
    w_at = lax.broadcasted_iota(jnp.int32, (wide, LANES), 0)
    inside1 = jnp.where(w_at < reach, jnp.where(has_up, 1.0, 0.0),
                        jnp.where(w_at >= reach + rows, jnp.where(has_dn, 1.0, 0.0), 1.0)).astype(f32)
    col_no = (lax.broadcasted_iota(jnp.int32, (blocks, LANES), 0) * LANES
              + lax.broadcasted_iota(jnp.int32, (blocks, LANES), 1)).astype(f32)
    ys, yc = sincos(tilts[0, 1] * col_no)
    ecol[0] = yc
    ecol[1] = ys

    def rows_conv(fields, matrix, zh, zl, c):
        out_rows = matrix.shape[0] // 4
        x = jnp.concatenate([part for pair in fields for part in pair], axis=1)
        hi, lo = split(x)
        m = matrix[...]
        y = jnp.dot(m, hi, preferred_element_type=f32)
        y = y[:2 * out_rows] + y[2 * out_rows:] + jnp.dot(m[:2 * out_rows], lo, preferred_element_type=f32)
        for b in range(per):
            o = b * 2 * LANES
            re = y[:out_rows, o:o + LANES] - y[out_rows:, o + LANES:o + 2 * LANES]
            im = y[:out_rows, o + LANES:o + 2 * LANES] + y[out_rows:, o:o + LANES]
            h, l = split(jnp.concatenate([re, im], axis=1))
            zh[1 + c * per + b] = h
            zl[1 + c * per + b] = l

    def cols_conv(zh, zl, table, c):
        out_rows = zh.shape[1]
        parts = [z[pl.ds(c * per + m, per)].reshape(per * out_rows, 2 * LANES)
                 for z in (zh, zl) for m in range(3)]
        x = jnp.concatenate(parts + parts[:3], axis=1)
        y = jnp.dot(x, table[...], preferred_element_type=f32)
        y = y.reshape(per, out_rows, 2 * LANES)
        return [(y[b, :, :LANES], y[b, :, LANES:]) for b in range(per)]

    def forward_a(c):
        arriving(lambda side: p0_copy(side, c))
        arriving(lambda side: p1_copy(side, c))
        fields = []
        for b in range(per):
            n = c * per + b
            at = slice(n * LANES, (n + 1) * LANES)
            sn, cs = sincos(jnp.concatenate([p0h[0, :, at], phase[0, :, at], p0h[1, :, at]], axis=0))
            yc, ys = ecol[0, n:n + 1, :], ecol[1, n:n + 1, :]
            tr, ti = cs * yc - sn * ys, cs * ys + sn * yc
            ec, es = erow[0], erow[1]
            re, im = tr * ec - ti * es, tr * es + ti * ec
            w0s[n, :, :LANES] = re[2 * reach:2 * reach + rows]
            w0s[n, :, LANES:] = im[2 * reach:2 * reach + rows]
            fields.append((re, im))
            sn, cs = sincos(jnp.concatenate([p1h[0, :, at], phase[1, :, at], p1h[1, :, at]], axis=0))
            t1s[n, :, :LANES] = cs * inside1
            t1s[n, :, LANES:] = sn * inside1
        rows_conv(fields, rf64, zah, zal, c)

    def forward_b(c):
        fields = []
        for b, (re, im) in enumerate(cols_conv(zah, zal, wf, c)):
            n = c * per + b
            cs, sn = t1s[n, :, :LANES], t1s[n, :, LANES:]
            wr, wi = cs * re - sn * im, cs * im + sn * re
            w1s[n, :, :LANES] = wr[reach:reach + rows]
            w1s[n, :, LANES:] = wi[reach:reach + rows]
            fields.append((wr, wi))
        rows_conv(fields, rf32, zbh, zbl, c)

    def forward_c(c):
        for b, (re, im) in enumerate(cols_conv(zbh, zbl, wf, c)):
            n = c * per + b
            at = slice(n * LANES, (n + 1) * LANES)
            lam[n, :, :LANES] = re - meas[0, 0, :, at]
            lam[n, :, LANES:] = im - meas[0, 1, :, at]
        sending(lambda side: l_copy(side, c))

    def backward_a(c):
        arriving(lambda side: l_copy(side, c))
        fields = []
        for b in range(per):
            n = c * per + b
            x = jnp.concatenate([lamh[0, n], lam[n], lamh[1, n]], axis=0)
            fields.append((x[:, :LANES], x[:, LANES:]))
        rows_conv(fields, rb64, zch, zcl, c)

    def send_terms(k, c):
        for p in range(c * pieces_per_chunk, (c + 1) * pieces_per_chunk):
            @pl.when(q != p)
            def _():
                g_copy(k, p).start()

            @pl.when(q == p)
            def _():
                rsr[q, k] = gs[k, p * piece:(p + 1) * piece]

    def backward_b(c):
        fields = []
        for b, (re, im) in enumerate(cols_conv(zch, zcl, wb, c)):
            n = c * per + b
            own = slice(reach, reach + rows)
            gs[1, n] = w1s[n, :, :LANES] * im[own] - w1s[n, :, LANES:] * re[own]
            cs, sn = t1s[n, :, :LANES], t1s[n, :, LANES:]
            fields.append((cs * re + sn * im, cs * im - sn * re))
        send_terms(1, c)
        rows_conv(fields, rb32, zdh, zdl, c)

    def backward_c(c):
        for b, (re, im) in enumerate(cols_conv(zdh, zdl, wb, c)):
            n = c * per + b
            gs[0, n] = w0s[n, :, :LANES] * im - w0s[n, :, LANES:] * re
        send_terms(0, c)

    for stages in ((forward_a, forward_b, forward_c), (backward_a, backward_b, backward_c)):
        for step in range(chunks + 2):
            for lag, stage in enumerate(stages):
                if 0 <= step - lag < chunks:
                    stage(step - lag)

    for k in (1, 0):
        for j in range(n_angle):
            @pl.when(q != j)
            def _():
                g_arrival(k, j).wait_recv()
        total = rsr[0, k]
        for j in range(1, n_angle):
            total = total + rsr[j, k]
        for b in range(piece):
            out[k, :, b * LANES:(b + 1) * LANES] = total[b]

    for c in range(chunks):
        sent(lambda side: p0_copy(side, c))
        sent(lambda side: p1_copy(side, c))
        sent(lambda side: l_copy(side, c))
    for k in (0, 1):
        for p in range(n_angle):
            @pl.when(q != p)
            def _():
                g_copy(k, p).wait_send()


def body(n_space, n_angle, phase_delay, measured, tilts, fresnel_taps):
    slices, rows, cols = phase_delay.shape
    reach = (fresnel_taps.shape[2] - 1) // 2
    blocks = cols // LANES
    chunks = 4
    wide, widest = rows + 2 * reach, rows + 4 * reach
    piece = blocks // n_angle
    vmem = pltpu.VMEM
    dma = pltpu.SemaphoreType.DMA
    scratch = [
        vmem((2, rows, cols), f32), vmem((2, reach, cols), f32),
        vmem((2, widest, LANES), f32), vmem((2, blocks, LANES), f32),
        vmem((blocks, wide, 2 * LANES), f32),
        vmem((blocks, rows, 2 * LANES), f32), vmem((blocks, rows, 2 * LANES), f32),
    ]
    for height in (wide, rows, wide, rows):
        scratch += [vmem((blocks + 2, height, 2 * LANES), bf16)] * 2
    scratch += [
        vmem((9 * 256, 256), bf16), vmem((9 * 256, 256), bf16),
        vmem((4 * wide, widest), bf16), vmem((4 * rows, wide), bf16),
        vmem((4 * wide, widest), bf16), vmem((4 * rows, wide), bf16),
        vmem((blocks, rows, 2 * LANES), f32), vmem((2, blocks, rows, 2 * LANES), f32),
        vmem((2, blocks, rows, LANES), f32), vmem((n_angle, 2, piece, rows, LANES), f32),
    ]
    scratch += [dma((2, chunks))] * 6 + [dma((2, n_angle))] * 2
    in_vmem = pl.BlockSpec(memory_space=pltpu.VMEM)
    in_smem = pl.BlockSpec(memory_space=pltpu.SMEM)
    return pl.pallas_call(
        functools.partial(kernel, (n_space, n_angle, chunks)),
        out_shape=jax.ShapeDtypeStruct((slices, rows, cols // n_angle), f32),
        in_specs=[in_vmem, in_vmem, in_smem, in_smem],
        out_specs=in_vmem,
        scratch_shapes=scratch,
        compiler_params=pltpu.CompilerParams(
            collective_id=0, has_side_effects=True, vmem_limit_bytes=48 * 1024 * 1024),
    )(phase_delay, measured, tilts, fresnel_taps)


def solution(mesh):
    return jax.shard_map(
        functools.partial(body, mesh.shape["space"], mesh.shape["angle"]),
        mesh=mesh,
        in_specs=(P(None, "space", None), P("angle", None, "space", None), P("angle", None), P()),
        out_specs=P(None, "space", "angle"),
        check_vma=False,
    )
```

time: 118 us -> 41.1 us (0.35)
  the two profiles are of different devices: /device:TPU:0 before, /device:TPU:27 now
where the time goes in v1:
time: 41.1 us; the launch traced here: 40.9 us
  Pallas kernels  36.8 us (90%)
  local copies, waits for them, and re-layouts  4.08 us (10%)
    pallas_call x1, Pallas kernels, body(): pl.pallas_call(functools.partial(kernel, (n_space, n_angle, chunks)), out...  36.8 us
    unnamed x9, local copies, waits for them, and re-layouts  4.08 us

profile of v1, /device:TPU:27, one launch (start us, length us, event | category | flops | bytes accessed | tf_op | source)
XLA Modules:
  0.0 40.9 jit_solution(13919311605253483570)
XLA Ops:
  0.0 0.0 copy-start
  0.0 1.0 %copy-done = f32[2,32,2048]{2,1,0:T(8,128)S(1)} copy-done((f32[2,32,2048]{2,1,0:T(8,128)S(1)}, f32[2,32,2048]{2,1,0:T(8,128)}, u32[]{:S(2)}) %copy-start) | copy-done | bytes 524312
  1.0 0.0 copy-start.1
  1.0 1.0 %copy-done.1 = f32[1,2,32,2048]{3,2,1,0:T(8,128)S(1)} copy-done((f32[1,2,32,2048]{3,2,1,0:T(8,128)S(1)}, f32[1,2,32,2048]{3,2,1,0:T(8,128)}, u32[]{:S(2)}) %copy-start.1) | copy-done | bytes 524312
  2.1 0.0 copy-start.2
  2.1 0.7 %copy-done.2 = f32[2,2,33]{2,1,0:T(2,128)S(1)} copy-done((f32[2,2,33]{2,1,0:T(2,128)S(1)}, f32[2,2,33]{2,1,0:T(2,128)}, u32[]{:S(2)}) %copy-start.2) | copy-done | bytes 552
  2.8 0.0 copy-start.3
  2.8 0.7 %copy-done.3 = f32[1,2]{1,0:T(1,128)S(1)} copy-done((f32[1,2]{1,0:T(1,128)S(1)}, f32[1,2]{1,0:T(1,128)}, u32[]{:S(2)}) %copy-start.3) | copy-done | bytes 32
  3.4 36.8 %shard_map.46 = f32[2,32,512]{2,1,0:T(8,128)S(1)} custom-call(f32[2,32,2048]{2,1,0:T(8,128)S(1)} %copy-done, f32[1,2,32,2048]{3,2,1,0:T(8,128)S(1)} %copy-done.1, f32[1,2]{1,0:T(1,128)S(1)} %copy-done.3, f32[2,2,33]{2,1,0:T(2,128)S(1)} %copy-done.2), custom_call_target="tpu_custom_call" | custom-call | tf_op jit(solution)/shard_map/pallas_call | solution.py:366
  40.2 0.7 %copy.6 = f32[2,32,512]{2,1,0:T(8,128)} copy(f32[2,32,512]{2,1,0:T(8,128)S(1)} %shard_map.46) | data formatting | bytes 262144
Async XLA Ops:
  0.0 1.0 %copy-start = (f32[2,32,2048]{2,1,0:T(8,128)S(1)}, f32[2,32,2048]{2,1,0:T(8,128)}, u32[]{:S(2)}) copy-start(f32[2,32,2048]{2,1,0:T(8,128)} %phase.1) | copy-start | bytes 1572868
  1.0 1.0 %copy-start.1 = (f32[1,2,32,2048]{3,2,1,0:T(8,128)S(1)}, f32[1,2,32,2048]{3,2,1,0:T(8,128)}, u32[]{:S(2)}) copy-start(f32[1,2,32,2048]{3,2,1,0:T(8,128)} %meas.1) | copy-start | bytes 1572868
  2.1 0.7 %copy-start.2 = (f32[2,2,33]{2,1,0:T(2,128)S(1)}, f32[2,2,33]{2,1,0:T(2,128)}, u32[]{:S(2)}) copy-start(f32[2,2,33]{2,1,0:T(2,128)} %taps.1) | copy-start | bytes 1588
  2.8 0.7 %copy-start.3 = (f32[1,2]{1,0:T(1,128)S(1)}, f32[1,2]{1,0:T(1,128)}, u32[]{:S(2)}) copy-start(f32[1,2]{1,0:T(1,128)} %tilts.1) | copy-start | bytes 28

commit v2 on v1

--- a/solution.py
+++ b/solution.py
@@ -33,10 +33,10 @@
 
 
 def kernel(
-    sizes, phase, meas, tilts, taps, out,
+    sizes, phase_in, meas_in, tilts_in, taps_in, out, phase, meas, tilts, taps,
     p0h, p1h, erow, ecol, t1s, w0s, w1s, zah, zal, zbh, zbl, zch, zcl, zdh, zdl,
     wf, wb, rf64, rf32, rb64, rb32, lam, lamh, gs, rsr,
-    p0_send, p0_recv, p1_send, p1_recv, l_send, l_recv, g_send, g_recv,
+    p0_send, p0_recv, p1_send, p1_recv, l_send, l_recv, g_send, g_recv, load,
 ):
     n_space, n_angle, chunks = sizes
     rows, cols = phase.shape[1], phase.shape[2]
@@ -56,6 +56,11 @@
     up_id = (jnp.maximum(s - 1, 0), q)
     dn_id = (jnp.minimum(s + 1, n_space - 1), q)
 
+    loads = [pltpu.make_async_copy(a, b, load.at[i]) for i, (a, b) in enumerate(
+        ((taps_in, taps), (tilts_in, tilts), (phase_in, phase), (meas_in, meas)))]
+    for copy in loads:
+        copy.start()
+
     barrier = pltpu.get_barrier_semaphore()
 
     @pl.when(has_up)
@@ -77,14 +82,14 @@
     def p0_copy(side, c):
         at = pl.ds(c * width, width)
         return pltpu.make_async_remote_copy(
-            phase.at[0, :, at], p0h.at[side, :, at], p0_send.at[side, c], p0_recv.at[side, c],
+            phase_in.at[0, :, at], p0h.at[side, :, at], p0_send.at[side, c], p0_recv.at[side, c],
             device_id=dn_id if side == 0 else up_id, device_id_type=MESH)
 
     def p1_copy(side, c):
         at = pl.ds(c * width, width)
         first = rows - reach if side == 0 else 0
         return pltpu.make_async_remote_copy(
-            phase.at[1, pl.ds(first, reach), at], p1h.at[side, :, at], p1_send.at[side, c], p1_recv.at[side, c],
+            phase_in.at[1, pl.ds(first, reach), at], p1h.at[side, :, at], p1_send.at[side, c], p1_recv.at[side, c],
             device_id=dn_id if side == 0 else up_id, device_id_type=MESH)
 
     def l_copy(side, c):
@@ -150,6 +155,7 @@
         ref[0] = jnp.zeros(ref.shape[1:], bf16)
         ref[blocks + 1] = jnp.zeros(ref.shape[1:], bf16)
 
+    loads[0].wait()
     src = lax.broadcasted_iota(jnp.int32, (LANES, LANES), 0)
     dst = lax.broadcasted_iota(jnp.int32, (LANES, LANES), 1)
     away = dst - src
@@ -178,21 +184,23 @@
     zr = jnp.zeros((wide, LANES), f32)
     cr, ci, br, bi, rr, ri, ar, ai = lax.fori_loop(
         0, n_taps, build, (zc, zc, zc, zc, zr, zr, zr, zr))
-    masks = (away <= reach - LANES, jnp.abs(away) <= reach, away >= LANES - reach)
+    near = jnp.abs(away) <= reach
+    masks = (near, jnp.abs(away) >= LANES - reach)
     for table, real, imag in ((wf, cr, ci), (wb, br, bi)):
         for m, mask in enumerate(masks):
             re, im = jnp.where(mask, real, 0.0), jnp.where(mask, imag, 0.0)
             hi, lo = split(jnp.concatenate(
                 [jnp.concatenate([re, im], axis=1), jnp.concatenate([-im, re], axis=1)], axis=0))
             table[pl.ds(256 * m, 256)] = hi
-            table[pl.ds(256 * (m + 3), 256)] = hi
-            table[pl.ds(256 * (m + 6), 256)] = lo
+            table[pl.ds(256 * (m + 2), 256)] = hi
+            table[pl.ds(256 * (m + 4), 256)] = lo
     for big, small, real, imag in ((rf64, rf32, rr, ri), (rb64, rb32, ar, ai)):
         rh, rl = split(real)
         ih, il = split(imag)
         big[...] = jnp.concatenate([rh, ih, rl, il], axis=0)[:, :widest]
         small[...] = jnp.concatenate([rh[:rows], ih[:rows], rl[:rows], il[:rows]], axis=0)[:, :wide]
 
+    loads[1].wait()
     row_at = lax.broadcasted_iota(jnp.int32, (widest, LANES), 0)
     row_no = (s * rows - 2 * reach + row_at).astype(f32)
     es, ec = sincos(tilts[0, 0] * row_no)
@@ -226,16 +234,19 @@
 
     def cols_conv(zh, zl, table, c):
         out_rows = zh.shape[1]
-        parts = [z[pl.ds(c * per + m, per)].reshape(per * out_rows, 2 * LANES)
-                 for z in (zh, zl) for m in range(3)]
-        x = jnp.concatenate(parts + parts[:3], axis=1)
+        lane = lax.broadcasted_iota(jnp.int32, (per, out_rows, 2 * LANES), 2)
+        after = jnp.bitwise_and(lane, LANES - 1) < LANES // 2
+        parts = []
+        for z in (zh, zl):
+            parts.append(z[pl.ds(c * per + 1, per)])
+            parts.append(jnp.where(after, z[pl.ds(c * per + 2, per)], z[pl.ds(c * per, per)]))
+        parts = [part.reshape(per * out_rows, 2 * LANES) for part in parts]
+        x = jnp.concatenate(parts + parts[:2], axis=1)
         y = jnp.dot(x, table[...], preferred_element_type=f32)
         y = y.reshape(per, out_rows, 2 * LANES)
         return [(y[b, :, :LANES], y[b, :, LANES:]) for b in range(per)]
 
     def forward_a(c):
-        arriving(lambda side: p0_copy(side, c))
-        arriving(lambda side: p1_copy(side, c))
         fields = []
         for b in range(per):
             n = c * per + b
@@ -270,10 +281,8 @@
             at = slice(n * LANES, (n + 1) * LANES)
             lam[n, :, :LANES] = re - meas[0, 0, :, at]
             lam[n, :, LANES:] = im - meas[0, 1, :, at]
-        sending(lambda side: l_copy(side, c))
 
     def backward_a(c):
-        arriving(lambda side: l_copy(side, c))
         fields = []
         for b in range(per):
             n = c * per + b
@@ -299,20 +308,39 @@
             gs[1, n] = w1s[n, :, :LANES] * im[own] - w1s[n, :, LANES:] * re[own]
             cs, sn = t1s[n, :, :LANES], t1s[n, :, LANES:]
             fields.append((cs * re + sn * im, cs * im - sn * re))
-        send_terms(1, c)
         rows_conv(fields, rb32, zdh, zdl, c)
 
     def backward_c(c):
         for b, (re, im) in enumerate(cols_conv(zdh, zdl, wb, c)):
             n = c * per + b
             gs[0, n] = w0s[n, :, :LANES] * im - w0s[n, :, LANES:] * re
-        send_terms(0, c)
-
-    for stages in ((forward_a, forward_b, forward_c), (backward_a, backward_b, backward_c)):
-        for step in range(chunks + 2):
-            for lag, stage in enumerate(stages):
-                if 0 <= step - lag < chunks:
-                    stage(step - lag)
+
+    loads[2].wait()
+    for step in range(chunks + 2):
+        if step < chunks:
+            arriving(lambda side: p0_copy(side, step))
+            arriving(lambda side: p1_copy(side, step))
+            forward_a(step)
+        if 0 <= step - 1 < chunks:
+            forward_b(step - 1)
+        if step == 2:
+            loads[3].wait()
+        if 0 <= step - 2:
+            forward_c(step - 2)
+            sending(lambda side: l_copy(side, step - 2))
+
+    for step in range(chunks + 2):
+        if step < chunks:
+            arriving(lambda side: l_copy(side, step))
+            backward_a(step)
+        if 0 <= step - 1 < chunks:
+            backward_b(step - 1)
+        if 0 <= step - 2:
+            backward_c(step - 2)
+        if 0 <= step - 1 < chunks:
+            send_terms(1, step - 1)
+        if 0 <= step - 2:
+            send_terms(0, step - 2)
 
     for k in (1, 0):
         for j in range(n_angle):
@@ -346,6 +374,8 @@
     vmem = pltpu.VMEM
     dma = pltpu.SemaphoreType.DMA
     scratch = [
+        vmem((slices, rows, cols), f32), vmem((1, 2, rows, cols), f32),
+        pltpu.SMEM(tilts.shape, f32), pltpu.SMEM(fresnel_taps.shape, f32),
         vmem((2, rows, cols), f32), vmem((2, reach, cols), f32),
         vmem((2, widest, LANES), f32), vmem((2, blocks, LANES), f32),
         vmem((blocks, wide, 2 * LANES), f32),
@@ -354,20 +384,19 @@
     for height in (wide, rows, wide, rows):
         scratch += [vmem((blocks + 2, height, 2 * LANES), bf16)] * 2
     scratch += [
-        vmem((9 * 256, 256), bf16), vmem((9 * 256, 256), bf16),
+        vmem((6 * 256, 256), bf16), vmem((6 * 256, 256), bf16),
         vmem((4 * wide, widest), bf16), vmem((4 * rows, wide), bf16),
         vmem((4 * wide, widest), bf16), vmem((4 * rows, wide), bf16),
         vmem((blocks, rows, 2 * LANES), f32), vmem((2, blocks, rows, 2 * LANES), f32),
         vmem((2, blocks, rows, LANES), f32), vmem((n_angle, 2, piece, rows, LANES), f32),
     ]
-    scratch += [dma((2, chunks))] * 6 + [dma((2, n_angle))] * 2
-    in_vmem = pl.BlockSpec(memory_space=pltpu.VMEM)
-    in_smem = pl.BlockSpec(memory_space=pltpu.SMEM)
+    scratch += [dma((2, chunks))] * 6 + [dma((2, n_angle))] * 2 + [dma((4,))]
+    in_hbm = pl.BlockSpec(memory_space=pltpu.HBM)
     return pl.pallas_call(
         functools.partial(kernel, (n_space, n_angle, chunks)),
         out_shape=jax.ShapeDtypeStruct((slices, rows, cols // n_angle), f32),
-        in_specs=[in_vmem, in_vmem, in_smem, in_smem],
-        out_specs=in_vmem,
+        in_specs=[in_hbm] * 4,
+        out_specs=pl.BlockSpec(memory_space=pltpu.VMEM),
         scratch_shapes=scratch,
         compiler_params=pltpu.CompilerParams(
             collective_id=0, has_side_effects=True, vmem_limit_bytes=48 * 1024 * 1024),

time: 41.1 us -> 40.3 us (0.981)
  Pallas kernels: 36.8 us -> 36 us
    pallas_call x1, Pallas kernels: 36.8 us -> 36 us  [body(): pl.pallas_call(functools.partial(kernel, (n_space, n_angle, chunks)), out...]
where the time goes in v2:
time: 40.3 us; the launch traced here: 40.1 us
  Pallas kernels  36 us (89%)
  local copies, waits for them, and re-layouts  4.08 us (10%)
    pallas_call x1, Pallas kernels, body(): pl.pallas_call(functools.partial(kernel, (n_space, n_angle, chunks)), out...  36 us
    unnamed x9, local copies, waits for them, and re-layouts  4.08 us

profile of v2, /device:TPU:27, one launch (start us, length us, event | category | flops | bytes accessed | tf_op | source)
XLA Modules:
  0.0 40.1 jit_solution(11289879078992288792)
XLA Ops:
  0.0 0.0 copy-start
  0.0 1.0 %copy-done = f32[2,32,2048]{2,1,0:T(8,128)S(1)} copy-done((f32[2,32,2048]{2,1,0:T(8,128)S(1)}, f32[2,32,2048]{2,1,0:T(8,128)}, u32[]{:S(2)}) %copy-start) | copy-done | bytes 524312
  1.0 0.0 copy-start.1
  1.0 1.0 %copy-done.1 = f32[1,2,32,2048]{3,2,1,0:T(8,128)S(1)} copy-done((f32[1,2,32,2048]{3,2,1,0:T(8,128)S(1)}, f32[1,2,32,2048]{3,2,1,0:T(8,128)}, u32[]{:S(2)}) %copy-start.1) | copy-done | bytes 524312
  2.1 0.0 copy-start.2
  2.1 0.7 %copy-done.2 = f32[2,2,33]{2,1,0:T(2,128)S(1)} copy-done((f32[2,2,33]{2,1,0:T(2,128)S(1)}, f32[2,2,33]{2,1,0:T(2,128)}, u32[]{:S(2)}) %copy-start.2) | copy-done | bytes 552
  2.8 0.0 copy-start.3
  2.8 0.7 %copy-done.3 = f32[1,2]{1,0:T(1,128)S(1)} copy-done((f32[1,2]{1,0:T(1,128)S(1)}, f32[1,2]{1,0:T(1,128)}, u32[]{:S(2)}) %copy-start.3) | copy-done | bytes 32
  3.4 36.0 %shard_map.46 = f32[2,32,512]{2,1,0:T(8,128)S(1)} custom-call(f32[2,32,2048]{2,1,0:T(8,128)S(1)} %copy-done, f32[1,2,32,2048]{3,2,1,0:T(8,128)S(1)} %copy-done.1, f32[1,2]{1,0:T(1,128)S(1)} %copy-done.3, f32[2,2,33]{2,1,0:T(2,128)S(1)} %copy-done.2), custom_call_target="tpu_custom_call" | custom-call | tf_op jit(solution)/shard_map/pallas_call | solution.py:395
  39.4 0.7 %copy.6 = f32[2,32,512]{2,1,0:T(8,128)} copy(f32[2,32,512]{2,1,0:T(8,128)S(1)} %shard_map.46) | data formatting | bytes 262144
Async XLA Ops:
  0.0 1.0 %copy-start = (f32[2,32,2048]{2,1,0:T(8,128)S(1)}, f32[2,32,2048]{2,1,0:T(8,128)}, u32[]{:S(2)}) copy-start(f32[2,32,2048]{2,1,0:T(8,128)} %phase_in.1) | copy-start | bytes 1572868
  1.0 1.0 %copy-start.1 = (f32[1,2,32,2048]{3,2,1,0:T(8,128)S(1)}, f32[1,2,32,2048]{3,2,1,0:T(8,128)}, u32[]{:S(2)}) copy-start(f32[1,2,32,2048]{3,2,1,0:T(8,128)} %meas_in.1) | copy-start | bytes 1572868
  2.1 0.7 %copy-start.2 = (f32[2,2,33]{2,1,0:T(2,128)S(1)}, f32[2,2,33]{2,1,0:T(2,128)}, u32[]{:S(2)}) copy-start(f32[2,2,33]{2,1,0:T(2,128)} %taps_in.1) | copy-start | bytes 1588
  2.8 0.7 %copy-start.3 = (f32[1,2]{1,0:T(1,128)S(1)}, f32[1,2]{1,0:T(1,128)}, u32[]{:S(2)}) copy-start(f32[1,2]{1,0:T(1,128)} %tilts_in.1) | copy-start | bytes 28

commit v3 on v2

--- a/solution.py
+++ b/solution.py
@@ -399,7 +399,7 @@
         out_specs=pl.BlockSpec(memory_space=pltpu.VMEM),
         scratch_shapes=scratch,
         compiler_params=pltpu.CompilerParams(
-            collective_id=0, has_side_effects=True, vmem_limit_bytes=48 * 1024 * 1024),
+            collective_id=0, has_side_effects=True, vmem_limit_bytes=62 * 1024 * 1024),
     )(phase_delay, measured, tilts, fresnel_taps)
 
 

time: 40.3 us -> 38.4 us (0.953)
  local copies, waits for them, and re-layouts: 4.08 us -> 1.57 us
  Pallas kernels: 36 us -> 36.7 us
    unnamed x9 -> x1, local copies, waits for them, and re-layouts: 4.08 us -> 1.57 us
    pallas_call x1, Pallas kernels: 36 us -> 36.7 us  [body(): pl.pallas_call(functools.partial(kernel, (n_space, n_angle, chunks)), out...]
where the time goes in v3:
time: 38.4 us; the launch traced here: 38.3 us
  Pallas kernels  36.7 us (96%)
  local copies, waits for them, and re-layouts  1.57 us (4%)
    pallas_call x1, Pallas kernels, body(): pl.pallas_call(functools.partial(kernel, (n_space, n_angle, chunks)), out...  36.7 us
    unnamed x1, local copies, waits for them, and re-layouts  1.57 us

profile of v3, /device:TPU:27, one launch (start us, length us, event | category | flops | bytes accessed | tf_op | source)
XLA Modules:
  0.0 38.3 jit_solution(5096384095444365919)
XLA Ops:
  0.0 36.7 %shard_map.46 = f32[2,32,512]{2,1,0:T(8,128)} custom-call(f32[2,32,2048]{2,1,0:T(8,128)} %phase_in.1, f32[1,2,32,2048]{3,2,1,0:T(8,128)} %meas_in.1, f32[1,2]{1,0:T(1,128)} %tilts_in.1, f32[2,2,33]{2,1,0:T(2,128)} %taps_in.1), custom_call_target="tpu_custom_call" | custom-call | tf_op jit(solution)/shard_map/pallas_call | solution.py:395
  36.7 1.6 %copy.6 = f32[2,32,512]{2,1,0:T(8,128)} copy(f32[2,32,512]{2,1,0:T(8,128)} %shard_map.46) | data formatting | bytes 262144

commit v4 on v3

--- a/solution.py
+++ b/solution.py
@@ -37,6 +37,7 @@
     p0h, p1h, erow, ecol, t1s, w0s, w1s, zah, zal, zbh, zbl, zch, zcl, zdh, zdl,
     wf, wb, rf64, rf32, rb64, rb32, lam, lamh, gs, rsr,
     p0_send, p0_recv, p1_send, p1_recv, l_send, l_recv, g_send, g_recv, load,
+    held0, held1, heldl, ra_send, ra_recv, rb_send, rb_recv,
 ):
     n_space, n_angle, chunks = sizes
     rows, cols = phase.shape[1], phase.shape[2]
@@ -61,7 +62,26 @@
     for copy in loads:
         copy.start()
 
+    relayed = n_space == 8
+    mid = n_space // 2
+    upper, lower = s == mid - 1, s == mid
+    relays = (n_space - 1, 0)
+    if relayed:
+        from_up, from_dn = has_up & (s != mid), has_dn & (s != mid - 1)
+    else:
+        from_up, from_dn = has_up, has_dn
+
     barrier = pltpu.get_barrier_semaphore()
+    if relayed:
+        for strip in relays:
+            @pl.when(upper | lower)
+            def _():
+                pl.semaphore_signal(barrier, inc=1, device_id=(jnp.int32(strip), q), device_id_type=MESH)
+
+            @pl.when(s == strip)
+            def _():
+                for middle in (mid - 1, mid):
+                    pl.semaphore_signal(barrier, inc=1, device_id=(jnp.int32(middle), q), device_id_type=MESH)
 
     @pl.when(has_up)
     def _():
@@ -77,6 +97,8 @@
             pl.semaphore_signal(barrier, inc=1, device_id=(s, jnp.int32(j)), device_id_type=MESH)
 
     expected = n_angle - 1 + jnp.where(has_up, 1, 0) + jnp.where(has_dn, 1, 0)
+    if relayed:
+        expected = expected + jnp.where(upper | lower | (s == 0) | (s == n_space - 1), 2, 0)
     pl.semaphore_wait(barrier, expected)
 
     def p0_copy(side, c):
@@ -108,36 +130,102 @@
             gs.at[k, pl.ds(0, piece)], rsr.at[j, k], g_send.at[k, 0], g_recv.at[k, j],
             device_id=(s, jnp.int32(j)), device_id_type=MESH)
 
-    def sending(make):
-        @pl.when(has_dn)
+    half = per // 2
+    lanes = width // 2
+
+    def parts_of(kind, d, h, c):
+        if kind == 2:
+            at, mine = pl.ds(c * per + h * half, half), pl.ds(c * half, half)
+            return lam.at[at], heldl.at[d, mine], lamh.at[d, at]
+        at, mine = pl.ds(c * width + h * lanes, lanes), pl.ds(c * lanes, lanes)
+        if kind == 0:
+            return phase_in.at[0, :, at], held0.at[d, :, mine], p0h.at[d, :, at]
+        first = rows - reach if d == 0 else 0
+        return phase_in.at[1, pl.ds(first, reach), at], held1.at[d, :, mine], p1h.at[d, :, at]
+
+    def to_relay(kind, d, h, c):
+        a, b, _ = parts_of(kind, d, h, c)
+        return pltpu.make_async_remote_copy(
+            a, b, ra_send.at[kind, h, c], ra_recv.at[kind, d, c],
+            device_id=(jnp.int32(relays[h]), q), device_id_type=MESH)
+
+    def from_relay(kind, d, h, c):
+        _, b, e = parts_of(kind, d, h, c)
+        return pltpu.make_async_remote_copy(
+            b, e, rb_send.at[kind, d, c], rb_recv.at[kind, h, c],
+            device_id=(jnp.int32(mid if d == 0 else mid - 1), q), device_id_type=MESH)
+
+    def middle(d):
+        return upper if d == 0 else lower
+
+    def relay(kinds):
+        if not relayed:
+            return
+        for h in range(2):
+            @pl.when(s == relays[h])
+            def _():
+                for c in range(chunks):
+                    for d in range(2):
+                        for kind in kinds:
+                            to_relay(kind, d, h, c).wait_recv()
+                            from_relay(kind, d, h, c).start()
+
+    def sending(make, kind, c):
+        @pl.when(from_dn)
         def _():
             make(0).start()
 
-        @pl.when(has_up)
+        @pl.when(from_up)
         def _():
             make(1).start()
 
-    def arriving(make):
-        @pl.when(has_up)
+        if relayed:
+            for d in range(2):
+                @pl.when(middle(d))
+                def _():
+                    for h in range(2):
+                        to_relay(kind, d, h, c).start()
+
+    def arriving(make, kind, c):
+        @pl.when(from_up)
         def _():
             make(0).wait_recv()
 
-        @pl.when(has_dn)
+        @pl.when(from_dn)
         def _():
             make(1).wait_recv()
 
-    def sent(make):
-        @pl.when(has_dn)
+        if relayed:
+            for d in range(2):
+                @pl.when(middle(1 - d))
+                def _():
+                    for h in range(2):
+                        from_relay(kind, d, h, c).wait_recv()
+
+    def sent(make, kind, c):
+        @pl.when(from_dn)
         def _():
             make(0).wait_send()
 
-        @pl.when(has_up)
+        @pl.when(from_up)
         def _():
             make(1).wait_send()
 
+        if relayed:
+            for d in range(2):
+                @pl.when(middle(d))
+                def _():
+                    for h in range(2):
+                        to_relay(kind, d, h, c).wait_send()
+            for h in range(2):
+                @pl.when(s == relays[h])
+                def _():
+                    for d in range(2):
+                        from_relay(kind, d, h, c).wait_send()
+
     for c in range(chunks):
-        sending(lambda side: p0_copy(side, c))
-        sending(lambda side: p1_copy(side, c))
+        sending(lambda side: p0_copy(side, c), 0, c)
+        sending(lambda side: p1_copy(side, c), 1, c)
 
     @pl.when(jnp.logical_not(has_up))
     def _():
@@ -315,11 +403,12 @@
             n = c * per + b
             gs[0, n] = w0s[n, :, :LANES] * im - w0s[n, :, LANES:] * re
 
+    relay((0, 1))
     loads[2].wait()
     for step in range(chunks + 2):
         if step < chunks:
-            arriving(lambda side: p0_copy(side, step))
-            arriving(lambda side: p1_copy(side, step))
+            arriving(lambda side: p0_copy(side, step), 0, step)
+            arriving(lambda side: p1_copy(side, step), 1, step)
             forward_a(step)
         if 0 <= step - 1 < chunks:
             forward_b(step - 1)
@@ -327,11 +416,12 @@
             loads[3].wait()
         if 0 <= step - 2:
             forward_c(step - 2)
-            sending(lambda side: l_copy(side, step - 2))
-
+            sending(lambda side: l_copy(side, step - 2), 2, step - 2)
+
+    relay((2,))
     for step in range(chunks + 2):
         if step < chunks:
-            arriving(lambda side: l_copy(side, step))
+            arriving(lambda side: l_copy(side, step), 2, step)
             backward_a(step)
         if 0 <= step - 1 < chunks:
             backward_b(step - 1)
@@ -354,9 +444,9 @@
             out[k, :, b * LANES:(b + 1) * LANES] = total[b]
 
     for c in range(chunks):
-        sent(lambda side: p0_copy(side, c))
-        sent(lambda side: p1_copy(side, c))
-        sent(lambda side: l_copy(side, c))
+        sent(lambda side: p0_copy(side, c), 0, c)
+        sent(lambda side: p1_copy(side, c), 1, c)
+        sent(lambda side: l_copy(side, c), 2, c)
     for k in (0, 1):
         for p in range(n_angle):
             @pl.when(q != p)
@@ -391,6 +481,10 @@
         vmem((2, blocks, rows, LANES), f32), vmem((n_angle, 2, piece, rows, LANES), f32),
     ]
     scratch += [dma((2, chunks))] * 6 + [dma((2, n_angle))] * 2 + [dma((4,))]
+    scratch += [
+        vmem((2, rows, cols // 2), f32), vmem((2, reach, cols // 2), f32),
+        vmem((2, blocks // 2, rows, 2 * LANES), f32),
+    ] + [dma((3, 2, chunks))] * 4
     in_hbm = pl.BlockSpec(memory_space=pltpu.HBM)
     return pl.pallas_call(
         functools.partial(kernel, (n_space, n_angle, chunks)),

time: 38.4 us -> 40.7 us (1.060)
  the two profiles are of different devices: /device:TPU:27 before, /device:TPU:31 now
where the time goes in v4:
time: 40.7 us; the launch traced here: 40.5 us
  Pallas kernels  39 us (96%)
  local copies, waits for them, and re-layouts  1.57 us (4%)
    pallas_call x1, Pallas kernels, body(): pl.pallas_call(functools.partial(kernel, (n_space, n_angle, chunks)), out...  39 us
    unnamed x1, local copies, waits for them, and re-layouts  1.57 us

profile of v4, /device:TPU:31, one launch (start us, length us, event | category | flops | bytes accessed | tf_op | source)
XLA Modules:
  0.0 40.5 jit_solution(5105055031384107920)
XLA Ops:
  0.0 39.0 %shard_map.46 = f32[2,32,512]{2,1,0:T(8,128)} custom-call(f32[2,32,2048]{2,1,0:T(8,128)} %phase_in.1, f32[1,2,32,2048]{3,2,1,0:T(8,128)} %meas_in.1, f32[1,2]{1,0:T(1,128)} %tilts_in.1, f32[2,2,33]{2,1,0:T(2,128)} %taps_in.1), custom_call_target="tpu_custom_call" | custom-call | tf_op jit(solution)/shard_map/pallas_call | solution.py:489
  39.0 1.6 %copy.6 = f32[2,32,512]{2,1,0:T(8,128)} copy(f32[2,32,512]{2,1,0:T(8,128)} %shard_map.46) | data formatting | bytes 262144

commit v5 on v3

--- a/solution.py
+++ b/solution.py
@@ -25,6 +25,21 @@
     for c in (-2.7557319e-7, 2.4801587e-5, -1.3888889e-3, 4.1666667e-2, -0.5, 1.0):
         c_ = c_ * z + f32(c)
     return sign * s * r, sign * c_
+
+
+def phase_sincos(x):
+    z = x * x
+    s = f32(9.984293181e-12)
+    for k in (-1.209355185e-08, 8.137806969e-06, -2.604165700e-03, 2.499999993e-01):
+        s = s * z + f32(k)
+    s = s * x
+    c = f32(3.553096396e-10)
+    for k in (-3.383580022e-07, 1.627510656e-04, -3.124995776e-02, 9.999999694e-01):
+        c = c * z + f32(k)
+    for _ in range(2):
+        d = s + s
+        s, c = d * c, f32(1.0) - d * s
+    return s, c
 
 
 def split(x):
@@ -156,34 +171,28 @@
         ref[blocks + 1] = jnp.zeros(ref.shape[1:], bf16)
 
     loads[0].wait()
-    src = lax.broadcasted_iota(jnp.int32, (LANES, LANES), 0)
-    dst = lax.broadcasted_iota(jnp.int32, (LANES, LANES), 1)
-    away = dst - src
-    turn = jnp.bitwise_and(away + LANES, LANES - 1)
-    r_out = lax.broadcasted_iota(jnp.int32, (wide, LANES), 0)
-    r_in = lax.broadcasted_iota(jnp.int32, (wide, LANES), 1)
-    r_away = r_out + reach - r_in
-
-    def build(step, carry):
-        cr, ci, br, bi, rr, ri, ar, ai = carry
+    group = 8
+    first = lax.broadcasted_iota(jnp.int32, (group, LANES), 0)
+    lane8 = lax.broadcasted_iota(jnp.int32, (group, LANES), 1)
+    turn = jnp.bitwise_and(lane8 - first + LANES, LANES - 1)
+    r_turn = jnp.bitwise_and(first + reach - lane8 + LANES, LANES - 1)
+    base = [jnp.zeros((group, LANES), f32)] * 8
+    for step in range(n_taps):
         a = step - reach
         hr, hi = taps[1, 0, step], taps[1, 1, step]
         gr, gi = taps[0, 0, step], taps[0, 1, step]
-        here = turn == jnp.bitwise_and(a + LANES, LANES - 1)
-        there = turn == jnp.bitwise_and(LANES - a, LANES - 1)
-        r_here = r_away == a
-        r_there = r_away == -a
-        return (
-            jnp.where(here, hr, cr), jnp.where(here, hi, ci),
-            jnp.where(there, hr, br), jnp.where(there, -hi, bi),
-            jnp.where(r_here, gr, rr), jnp.where(r_here, gi, ri),
-            jnp.where(r_there, gr, ar), jnp.where(r_there, -gi, ai),
-        )
-
-    zc = jnp.zeros((LANES, LANES), f32)
-    zr = jnp.zeros((wide, LANES), f32)
-    cr, ci, br, bi, rr, ri, ar, ai = lax.fori_loop(
-        0, n_taps, build, (zc, zc, zc, zc, zr, zr, zr, zr))
+        hits = (turn == a % LANES, turn == -a % LANES, r_turn == a % LANES, r_turn == -a % LANES)
+        values = (hr, hi, hr, -hi, gr, gi, gr, -gi)
+        base = [jnp.where(hits[i // 2], values[i], base[i]) for i in range(8)]
+
+    def circulant(x, count):
+        return jnp.concatenate(
+            [x] + [pltpu.roll(x, group * i, 1) for i in range(1, count // group)], axis=0)
+
+    cr, ci, br, bi = [circulant(x, LANES) for x in base[:4]]
+    rr, ri, ar, ai = [circulant(x, wide) for x in base[4:]]
+    away = (lax.broadcasted_iota(jnp.int32, (LANES, LANES), 1)
+            - lax.broadcasted_iota(jnp.int32, (LANES, LANES), 0))
     near = jnp.abs(away) <= reach
     masks = (near, jnp.abs(away) >= LANES - reach)
     for table, real, imag in ((wf, cr, ci), (wb, br, bi)):
@@ -195,10 +204,13 @@
             table[pl.ds(256 * (m + 2), 256)] = hi
             table[pl.ds(256 * (m + 4), 256)] = lo
     for big, small, real, imag in ((rf64, rf32, rr, ri), (rb64, rb32, ar, ai)):
-        rh, rl = split(real)
-        ih, il = split(imag)
-        big[...] = jnp.concatenate([rh, ih, rl, il], axis=0)[:, :widest]
-        small[...] = jnp.concatenate([rh[:rows], ih[:rows], rl[:rows], il[:rows]], axis=0)[:, :wide]
+        for table, out_rows, depth in ((big, wide, widest), (small, rows, wide)):
+            re, im = real[:out_rows, :depth], imag[:out_rows, :depth]
+            hi, lo = split(jnp.concatenate(
+                [jnp.concatenate([re, -im], axis=1), jnp.concatenate([im, re], axis=1)], axis=0))
+            table[:, :2 * depth] = hi
+            table[:, 2 * depth:4 * depth] = hi
+            table[:, 4 * depth:] = lo
 
     loads[1].wait()
     row_at = lax.broadcasted_iota(jnp.int32, (widest, LANES), 0)
@@ -218,17 +230,12 @@
     ecol[1] = ys
 
     def rows_conv(fields, matrix, zh, zl, c):
-        out_rows = matrix.shape[0] // 4
-        x = jnp.concatenate([part for pair in fields for part in pair], axis=1)
-        hi, lo = split(x)
-        m = matrix[...]
-        y = jnp.dot(m, hi, preferred_element_type=f32)
-        y = y[:2 * out_rows] + y[2 * out_rows:] + jnp.dot(m[:2 * out_rows], lo, preferred_element_type=f32)
+        out_rows = matrix.shape[0] // 2
+        hi, lo = split(jnp.concatenate([jnp.concatenate(part, axis=1) for part in zip(*fields)], axis=0))
+        y = jnp.dot(matrix[...], jnp.concatenate([hi, lo, hi], axis=0), preferred_element_type=f32)
         for b in range(per):
-            o = b * 2 * LANES
-            re = y[:out_rows, o:o + LANES] - y[out_rows:, o + LANES:o + 2 * LANES]
-            im = y[:out_rows, o + LANES:o + 2 * LANES] + y[out_rows:, o:o + LANES]
-            h, l = split(jnp.concatenate([re, im], axis=1))
+            at = slice(b * LANES, (b + 1) * LANES)
+            h, l = split(jnp.concatenate([y[:out_rows, at], y[out_rows:, at]], axis=1))
             zh[1 + c * per + b] = h
             zl[1 + c * per + b] = l
 
@@ -251,7 +258,7 @@
         for b in range(per):
             n = c * per + b
             at = slice(n * LANES, (n + 1) * LANES)
-            sn, cs = sincos(jnp.concatenate([p0h[0, :, at], phase[0, :, at], p0h[1, :, at]], axis=0))
+            sn, cs = phase_sincos(jnp.concatenate([p0h[0, :, at], phase[0, :, at], p0h[1, :, at]], axis=0))
             yc, ys = ecol[0, n:n + 1, :], ecol[1, n:n + 1, :]
             tr, ti = cs * yc - sn * ys, cs * ys + sn * yc
             ec, es = erow[0], erow[1]
@@ -259,7 +266,7 @@
             w0s[n, :, :LANES] = re[2 * reach:2 * reach + rows]
             w0s[n, :, LANES:] = im[2 * reach:2 * reach + rows]
             fields.append((re, im))
-            sn, cs = sincos(jnp.concatenate([p1h[0, :, at], phase[1, :, at], p1h[1, :, at]], axis=0))
+            sn, cs = phase_sincos(jnp.concatenate([p1h[0, :, at], phase[1, :, at], p1h[1, :, at]], axis=0))
             t1s[n, :, :LANES] = cs * inside1
             t1s[n, :, LANES:] = sn * inside1
         rows_conv(fields, rf64, zah, zal, c)
@@ -385,8 +392,8 @@
         scratch += [vmem((blocks + 2, height, 2 * LANES), bf16)] * 2
     scratch += [
         vmem((6 * 256, 256), bf16), vmem((6 * 256, 256), bf16),
-        vmem((4 * wide, widest), bf16), vmem((4 * rows, wide), bf16),
-        vmem((4 * wide, widest), bf16), vmem((4 * rows, wide), bf16),
+        vmem((2 * wide, 6 * widest), bf16), vmem((2 * rows, 6 * wide), bf16),
+        vmem((2 * wide, 6 * widest), bf16), vmem((2 * rows, 6 * wide), bf16),
         vmem((blocks, rows, 2 * LANES), f32), vmem((2, blocks, rows, 2 * LANES), f32),
         vmem((2, blocks, rows, LANES), f32), vmem((n_angle, 2, piece, rows, LANES), f32),
     ]

time: 38.4 us -> 37.9 us (0.987)
  Pallas kernels: 36.7 us -> 36.2 us
    pallas_call x1, Pallas kernels: 36.7 us -> 36.2 us  [body(): pl.pallas_call(functools.partial(kernel, (n_space, n_angle, chunks)), out...]
where the time goes in v5:
time: 37.9 us; the launch traced here: 37.7 us
  Pallas kernels  36.2 us (96%)
  local copies, waits for them, and re-layouts  1.57 us (4%)
    pallas_call x1, Pallas kernels, body(): pl.pallas_call(functools.partial(kernel, (n_space, n_angle, chunks)), out...  36.2 us
    unnamed x1, local copies, waits for them, and re-layouts  1.57 us

profile of v5, /device:TPU:27, one launch (start us, length us, event | category | flops | bytes accessed | tf_op | source)
XLA Modules:
  0.0 37.7 jit_solution(17862810108111221473)
XLA Ops:
  0.0 36.2 %shard_map.46 = f32[2,32,512]{2,1,0:T(8,128)} custom-call(f32[2,32,2048]{2,1,0:T(8,128)} %phase_in.1, f32[1,2,32,2048]{3,2,1,0:T(8,128)} %meas_in.1, f32[1,2]{1,0:T(1,128)} %tilts_in.1, f32[2,2,33]{2,1,0:T(2,128)} %taps_in.1), custom_call_target="tpu_custom_call" | custom-call | tf_op jit(solution)/shard_map/pallas_call | solution.py:402
  36.2 1.6 %copy.6 = f32[2,32,512]{2,1,0:T(8,128)} copy(f32[2,32,512]{2,1,0:T(8,128)} %shard_map.46) | data formatting | bytes 262144

commit v6 on v5

--- a/solution.py
+++ b/solution.py
@@ -40,6 +40,10 @@
         d = s + s
         s, c = d * c, f32(1.0) - d * s
     return s, c
+
+
+def lanes_at(start, size):
+    return pl.ds(start if isinstance(start, int) else pl.multiple_of(start, LANES), size)
 
 
 def split(x):
@@ -95,13 +99,13 @@
     pl.semaphore_wait(barrier, expected)
 
     def p0_copy(side, c):
-        at = pl.ds(c * width, width)
+        at = lanes_at(c * width, width)
         return pltpu.make_async_remote_copy(
             phase_in.at[0, :, at], p0h.at[side, :, at], p0_send.at[side, c], p0_recv.at[side, c],
             device_id=dn_id if side == 0 else up_id, device_id_type=MESH)
 
     def p1_copy(side, c):
-        at = pl.ds(c * width, width)
+        at = lanes_at(c * width, width)
         first = rows - reach if side == 0 else 0
         return pltpu.make_async_remote_copy(
             phase_in.at[1, pl.ds(first, reach), at], p1h.at[side, :, at], p1_send.at[side, c], p1_recv.at[side, c],
@@ -150,7 +154,11 @@
         def _():
             make(1).wait_send()
 
-    for c in range(chunks):
+    def turn_of(step):
+        return jnp.where(q < n_angle // 2, chunks - 1 - step, step)
+
+    for step in range(chunks):
+        c = turn_of(step)
         sending(lambda side: p0_copy(side, c))
         sending(lambda side: p1_copy(side, c))
 
@@ -257,9 +265,9 @@
         fields = []
         for b in range(per):
             n = c * per + b
-            at = slice(n * LANES, (n + 1) * LANES)
+            at = lanes_at(n * LANES, LANES)
             sn, cs = phase_sincos(jnp.concatenate([p0h[0, :, at], phase[0, :, at], p0h[1, :, at]], axis=0))
-            yc, ys = ecol[0, n:n + 1, :], ecol[1, n:n + 1, :]
+            yc, ys = ecol[0, pl.ds(n, 1), :], ecol[1, pl.ds(n, 1), :]
             tr, ti = cs * yc - sn * ys, cs * ys + sn * yc
             ec, es = erow[0], erow[1]
             re, im = tr * ec - ti * es, tr * es + ti * ec
@@ -285,7 +293,7 @@
     def forward_c(c):
         for b, (re, im) in enumerate(cols_conv(zbh, zbl, wf, c)):
             n = c * per + b
-            at = slice(n * LANES, (n + 1) * LANES)
+            at = lanes_at(n * LANES, LANES)
             lam[n, :, :LANES] = re - meas[0, 0, :, at]
             lam[n, :, LANES:] = im - meas[0, 1, :, at]
 
@@ -298,14 +306,16 @@
         rows_conv(fields, rb64, zch, zcl, c)
 
     def send_terms(k, c):
-        for p in range(c * pieces_per_chunk, (c + 1) * pieces_per_chunk):
+        for i in range(pieces_per_chunk):
+            p = c * pieces_per_chunk + i
+
             @pl.when(q != p)
             def _():
                 g_copy(k, p).start()
 
             @pl.when(q == p)
             def _():
-                rsr[q, k] = gs[k, p * piece:(p + 1) * piece]
+                rsr[q, k] = gs[k, pl.ds(p * piece, piece)]
 
     def backward_b(c):
         fields = []
@@ -323,31 +333,35 @@
             gs[0, n] = w0s[n, :, :LANES] * im - w0s[n, :, LANES:] * re
 
     loads[2].wait()
+    order = [turn_of(step) for step in range(chunks)]
     for step in range(chunks + 2):
         if step < chunks:
-            arriving(lambda side: p0_copy(side, step))
-            arriving(lambda side: p1_copy(side, step))
-            forward_a(step)
+            c = order[step]
+            arriving(lambda side: p0_copy(side, c))
+            arriving(lambda side: p1_copy(side, c))
+            forward_a(c)
         if 0 <= step - 1 < chunks:
-            forward_b(step - 1)
+            forward_b(order[step - 1])
         if step == 2:
             loads[3].wait()
         if 0 <= step - 2:
-            forward_c(step - 2)
-            sending(lambda side: l_copy(side, step - 2))
+            c = order[step - 2]
+            forward_c(c)
+            sending(lambda side: l_copy(side, c))
 
     for step in range(chunks + 2):
         if step < chunks:
-            arriving(lambda side: l_copy(side, step))
-            backward_a(step)
+            c = order[step]
+            arriving(lambda side: l_copy(side, c))
+            backward_a(c)
         if 0 <= step - 1 < chunks:
-            backward_b(step - 1)
+            backward_b(order[step - 1])
         if 0 <= step - 2:
-            backward_c(step - 2)
+            backward_c(order[step - 2])
         if 0 <= step - 1 < chunks:
-            send_terms(1, step - 1)
+            send_terms(1, order[step - 1])
         if 0 <= step - 2:
-            send_terms(0, step - 2)
+            send_terms(0, order[step - 2])
 
     for k in (1, 0):
         for j in range(n_angle):

time: 37.9 us -> 36 us (0.950)
  the two profiles are of different devices: /device:TPU:27 before, /device:TPU:4 now
where the time goes in v6:
time: 36 us; the launch traced here: 35.9 us
  Pallas kernels  34.3 us (95%)
  local copies, waits for them, and re-layouts  1.57 us (4%)
    pallas_call x1, Pallas kernels, body(): pl.pallas_call(functools.partial(kernel, (n_space, n_angle, chunks)), out...  34.3 us
    unnamed x1, local copies, waits for them, and re-layouts  1.57 us

profile of v6, /device:TPU:4, one launch (start us, length us, event | category | flops | bytes accessed | tf_op | source)
XLA Modules:
  0.0 35.9 jit_solution(2266916547801872333)
XLA Ops:
  0.0 34.3 %shard_map.46 = f32[2,32,512]{2,1,0:T(8,128)} custom-call(f32[2,32,2048]{2,1,0:T(8,128)} %phase_in.1, f32[1,2,32,2048]{3,2,1,0:T(8,128)} %meas_in.1, f32[1,2]{1,0:T(1,128)} %tilts_in.1, f32[2,2,33]{2,1,0:T(2,128)} %taps_in.1), custom_call_target="tpu_custom_call" | custom-call | tf_op jit(solution)/shard_map/pallas_call | solution.py:416
  34.3 1.6 %copy.6 = f32[2,32,512]{2,1,0:T(8,128)} copy(f32[2,32,512]{2,1,0:T(8,128)} %shard_map.46) | data formatting | bytes 262144

commit v7 on v6

--- a/solution.py
+++ b/solution.py
@@ -56,6 +56,7 @@
     p0h, p1h, erow, ecol, t1s, w0s, w1s, zah, zal, zbh, zbl, zch, zcl, zdh, zdl,
     wf, wb, rf64, rf32, rb64, rb32, lam, lamh, gs, rsr,
     p0_send, p0_recv, p1_send, p1_recv, l_send, l_recv, g_send, g_recv, load,
+    acc, acc_send, acc_recv,
 ):
     n_space, n_angle, chunks = sizes
     rows, cols = phase.shape[1], phase.shape[2]
@@ -127,6 +128,16 @@
             gs.at[k, pl.ds(0, piece)], rsr.at[j, k], g_send.at[k, 0], g_recv.at[k, j],
             device_id=(s, jnp.int32(j)), device_id_type=MESH)
 
+    paired = n_angle == 4 and chunks == 4
+    inner = (q > 0) & (q < n_angle - 1)
+    partner = q + 1 - 2 * lax.rem(q, 2)
+
+    def to_partner(k, p):
+        slot = lax.rem(p, 2)
+        return pltpu.make_async_remote_copy(
+            gs.at[k, pl.ds(p * piece, piece)], acc.at[k, slot], acc_send.at[k, slot], acc_recv.at[k, slot],
+            device_id=(s, partner), device_id_type=MESH)
+
     def sending(make):
         @pl.when(has_dn)
         def _():
@@ -157,8 +168,8 @@
     def turn_of(step):
         return jnp.where(q < n_angle // 2, chunks - 1 - step, step)
 
-    for step in range(chunks):
-        c = turn_of(step)
+    order = [turn_of(step) for step in range(chunks)]
+    for c in order:
         sending(lambda side: p0_copy(side, c))
         sending(lambda side: p1_copy(side, c))
 
@@ -305,7 +316,22 @@
             fields.append((x[:, :LANES], x[:, LANES:]))
         rows_conv(fields, rb64, zch, zcl, c)
 
-    def send_terms(k, c):
+    def send_on(k, c):
+        @pl.when(inner)
+        def _():
+            to_partner(k, c).wait_recv()
+            at = pl.ds(c * piece, piece)
+            gs[k, at] = gs[k, at] + acc[k, lax.rem(c, 2)]
+            g_copy(k, c).start()
+
+    def send_terms(k, step):
+        c = order[step]
+        if paired and step < 2:
+            @pl.when(jnp.logical_not(inner))
+            def _():
+                to_partner(k, c).start()
+
+            return
         for i in range(pieces_per_chunk):
             p = c * pieces_per_chunk + i
 
@@ -333,7 +359,6 @@
             gs[0, n] = w0s[n, :, :LANES] * im - w0s[n, :, LANES:] * re
 
     loads[2].wait()
-    order = [turn_of(step) for step in range(chunks)]
     for step in range(chunks + 2):
         if step < chunks:
             c = order[step]
@@ -359,18 +384,28 @@
         if 0 <= step - 2:
             backward_c(order[step - 2])
         if 0 <= step - 1 < chunks:
-            send_terms(1, order[step - 1])
+            send_terms(1, step - 1)
         if 0 <= step - 2:
-            send_terms(0, order[step - 2])
+            send_terms(0, step - 2)
+        if paired and 0 <= step - 2 < 2:
+            send_on(1, order[step - 2])
+        if paired and 0 <= step - 3 < 2:
+            send_on(0, order[step - 3])
 
     for k in (1, 0):
-        for j in range(n_angle):
-            @pl.when(q != j)
-            def _():
-                g_arrival(k, j).wait_recv()
-        total = rsr[0, k]
-        for j in range(1, n_angle):
-            total = total + rsr[j, k]
+        if paired:
+            across = jnp.where(q < 2, 2, 1)
+            g_arrival(k, partner).wait_recv()
+            g_arrival(k, across).wait_recv()
+            total = rsr[q, k] + rsr[partner, k] + rsr[across, k]
+        else:
+            for j in range(n_angle):
+                @pl.when(q != j)
+                def _():
+                    g_arrival(k, j).wait_recv()
+            total = rsr[0, k]
+            for j in range(1, n_angle):
+                total = total + rsr[j, k]
         for b in range(piece):
             out[k, :, b * LANES:(b + 1) * LANES] = total[b]
 
@@ -380,7 +415,19 @@
         sent(lambda side: l_copy(side, c))
     for k in (0, 1):
         for p in range(n_angle):
-            @pl.when(q != p)
+            if paired:
+                far = (q < 2) if p >= 2 else (q >= 2)
+                by_hand = far & jnp.logical_not(inner)
+
+                @pl.when(by_hand)
+                def _():
+                    to_partner(k, p).wait_send()
+
+                direct = (q != p) & jnp.logical_not(by_hand)
+            else:
+                direct = q != p
+
+            @pl.when(direct)
             def _():
                 g_copy(k, p).wait_send()
 
@@ -412,6 +459,7 @@
         vmem((2, blocks, rows, LANES), f32), vmem((n_angle, 2, piece, rows, LANES), f32),
     ]
     scratch += [dma((2, chunks))] * 6 + [dma((2, n_angle))] * 2 + [dma((4,))]
+    scratch += [vmem((2, 2, piece, rows, LANES), f32), dma((2, 2)), dma((2, 2))]
     in_hbm = pl.BlockSpec(memory_space=pltpu.HBM)
     return pl.pallas_call(
         functools.partial(kernel, (n_space, n_angle, chunks)),

time: 36 us -> 37.8 us (1.050)
  Pallas kernels: 34.3 us -> 36.1 us
    pallas_call x1, Pallas kernels: 34.3 us -> 36.1 us  [body(): pl.pallas_call(functools.partial(kernel, (n_space, n_angle, chunks)), out...]
where the time goes in v7:
time: 37.8 us; the launch traced here: 37.7 us
  Pallas kernels  36.1 us (96%)
  local copies, waits for them, and re-layouts  1.57 us (4%)
    pallas_call x1, Pallas kernels, body(): pl.pallas_call(functools.partial(kernel, (n_space, n_angle, chunks)), out...  36.1 us
    unnamed x1, local copies, waits for them, and re-layouts  1.57 us

profile of v7, /device:TPU:4, one launch (start us, length us, event | category | flops | bytes accessed | tf_op | source)
XLA Modules:
  0.0 37.7 jit_solution(18108870732842111664)
XLA Ops:
  0.0 36.1 %shard_map.46 = f32[2,32,512]{2,1,0:T(8,128)} custom-call(f32[2,32,2048]{2,1,0:T(8,128)} %phase_in.1, f32[1,2,32,2048]{3,2,1,0:T(8,128)} %meas_in.1, f32[1,2]{1,0:T(1,128)} %tilts_in.1, f32[2,2,33]{2,1,0:T(2,128)} %taps_in.1), custom_call_target="tpu_custom_call" | custom-call | tf_op jit(solution)/shard_map/pallas_call | solution.py:464
  36.1 1.6 %copy.6 = f32[2,32,512]{2,1,0:T(8,128)} copy(f32[2,32,512]{2,1,0:T(8,128)} %shard_map.46) | data formatting | bytes 262144

commit v8 on v6

--- a/solution.py
+++ b/solution.py
@@ -389,7 +389,7 @@
     slices, rows, cols = phase_delay.shape
     reach = (fresnel_taps.shape[2] - 1) // 2
     blocks = cols // LANES
-    chunks = 4
+    chunks = 2
     wide, widest = rows + 2 * reach, rows + 4 * reach
     piece = blocks // n_angle
     vmem = pltpu.VMEM

time: 36 us -> 42.1 us (1.17)
  the two profiles are of different devices: /device:TPU:4 before, /device:TPU:3 now
where the time goes in v8:
time: 42.1 us; the launch traced here: 42 us
  Pallas kernels  40.4 us (96%)
  local copies, waits for them, and re-layouts  1.57 us (4%)
    pallas_call x1, Pallas kernels, body(): pl.pallas_call(functools.partial(kernel, (n_space, n_angle, chunks)), out...  40.4 us
    unnamed x1, local copies, waits for them, and re-layouts  1.57 us

profile of v8, /device:TPU:3, one launch (start us, length us, event | category | flops | bytes accessed | tf_op | source)
XLA Modules:
  0.0 42.0 jit_solution(13496276342964235840)
XLA Ops:
  0.0 40.4 %shard_map.46 = f32[2,32,512]{2,1,0:T(8,128)} custom-call(f32[2,32,2048]{2,1,0:T(8,128)} %phase_in.1, f32[1,2,32,2048]{3,2,1,0:T(8,128)} %meas_in.1, f32[1,2]{1,0:T(1,128)} %tilts_in.1, f32[2,2,33]{2,1,0:T(2,128)} %taps_in.1), custom_call_target="tpu_custom_call" | custom-call | tf_op jit(solution)/shard_map/pallas_call | solution.py:416
  40.4 1.6 %copy.6 = f32[2,32,512]{2,1,0:T(8,128)} copy(f32[2,32,512]{2,1,0:T(8,128)} %shard_map.46) | data formatting | bytes 262144
